TPU v7x, 256 devices: a whole 4x4x8 slice. The times are simulated.
256 devices in a mesh: wide: 64 (over x_lo, z, y), narrow: 4 (over x_hi, core).
Axes of the slice: x: 4 (x_hi: 2, x_lo: 2; x = x_hi * 2 + x_lo), y: 4, z: 8, core: 2. Of those that a mesh axis runs over, the one named last changes fastest.
Arguments:
- field: bfloat16 [2, 512, 512, 512], P(None, 'wide', 'narrow'), may hold values from -20 to 20
- gain: float32 [512, 512], P('wide', 'narrow'), may hold values from 0.2 to 1
- spectral_phase: float32 [512], replicated, may hold values from -3.140625 to 3.140625
Outputs:
- field_out: bfloat16 [2, 512, 512, 512], P(None, 'wide', 'narrow')
All inputs are finite; a program needn't handle non-finite values.
Results may differ from a plain program's by a relative error of at most 0.017.
Values may be sent and summed in bfloat16 or wider, within the bound.
A program may use at most 64 MiB of HBM per device.

v0:
```python
import math

import jax
import jax.numpy as jnp
import numpy as np
from jax import lax
from jax.experimental import pallas as pl
from jax.experimental.pallas import tpu as pltpu
from jax.sharding import PartitionSpec as P

MESH = pl.DeviceIdType.MESH
BF16 = jnp.bfloat16
F32 = jnp.float32

N = 512
DEV = 256
WIDE = 64
NARROW = 4
ROWS = 8
COLS = 128
KERR = 0.25
SATURATION = 1.0
DIFFRACT = 120.0
ROW_STRIDE = DEV

def _fit(func, count):
    nodes = 0.125 * (1.0 - np.cos((np.arange(400) + 0.5) * np.pi / 400))
    powers = nodes[:, None] ** np.arange(count)[None, :]
    return [float(v) for v in np.linalg.lstsq(powers, func(np.sqrt(nodes)), rcond=None)[0]]


SIN_TERMS = _fit(lambda z: np.sin(2 * np.pi * z) / z, 7)
COS_TERMS = _fit(lambda z: np.cos(2 * np.pi * z), 7)


def horner(terms, value):
    total = terms[-1]
    for term in terms[-2::-1]:
        total = total * value + term
    return total


def dft_tables(count):
    index = np.arange(count)
    angle = (index[:, None] * index[None, :] % count) * (2.0 * math.pi / count)
    factor = 1.0 / math.sqrt(count)
    return np.cos(angle) * factor, np.sin(angle) * factor


def signed_freq(index, count):
    return np.where(index < count // 2, index, index - count) / count


def time_tables():
    cos_table, sin_table = dft_tables(N)
    forward = np.block([[cos_table, sin_table], [-sin_table, cos_table]])
    inverse = np.block([[cos_table, sin_table], [-sin_table, cos_table]])
    order = np.arange(2 * N).reshape(2, 2, DEV).transpose(1, 0, 2).reshape(-1)
    return forward[order].astype(BF16), inverse[order].astype(BF16)


def line_kernels():
    index = np.arange(N)
    wave = signed_freq(index, N)
    chirp = np.exp(-1j * DIFFRACT * (wave * wave)[None, :] / (1.0 + 0.5 * wave)[:, None])
    lines = np.fft.ifft(chirp, axis=1)
    return np.stack([lines.real, lines.imag], axis=1).reshape(N, 8, 128).astype(np.float32)


def kernel(
    field_hbm,
    gain_ref,
    phase_ref,
    forward_hbm,
    inverse_hbm,
    lines_hbm,
    out_ref,
    field,
    kerr,
    forward,
    inverse,
    lines,
    circ,
    gain_t,
    spread,
    send1,
    recv1,
    plane,
    send2,
    recv2,
    total,
    load_sem,
    send_sem,
    recv_sem,
):
    wide = lax.axis_index("wide")
    narrow = lax.axis_index("narrow")
    me = wide * NARROW + narrow
    place = narrow * WIDE + wide

    barrier = pltpu.get_barrier_semaphore()

    @pl.loop(1, DEV)
    def _(step):
        other = lax.rem(me + step, DEV)
        pl.semaphore_signal(
            barrier, inc=1, device_id=(other // NARROW, lax.rem(other, NARROW)), device_id_type=MESH
        )

    loads = [
        pltpu.make_async_copy(field_hbm, field, load_sem.at[0]),
        pltpu.make_async_copy(forward_hbm, forward, load_sem.at[1]),
        pltpu.make_async_copy(lines_hbm.at[pl.ds(me, 1)], lines.at[pl.ds(0, 1)], load_sem.at[2]),
        pltpu.make_async_copy(lines_hbm.at[pl.ds(DEV + me, 1)], lines.at[pl.ds(1, 1)], load_sem.at[3]),
        pltpu.make_async_copy(inverse_hbm, inverse, load_sem.at[4]),
    ]
    for load in loads:
        load.start()

    gain_t[...] = jnp.transpose(gain_ref[...])
    loads[0].wait()

    block = 32

    @pl.loop(0, ROWS * COLS // block)
    def _(step):
        row = step // (COLS // block)
        col = pl.multiple_of(lax.rem(step, COLS // block) * block, block)
        real = field[0, row, pl.ds(col, block), :].astype(F32)
        imag = field[1, row, pl.ds(col, block), :].astype(F32)
        intensity = real * real + imag * imag
        fluence = jnp.sum(intensity, axis=1, keepdims=True) * (1.0 / N)
        gains = gain_t[pl.ds(col, block), :]
        lane = lax.broadcasted_iota(jnp.int32, gains.shape, 1)
        gain = jnp.sum(jnp.where(lane == row, gains, 0.0), axis=1, keepdims=True)
        amplitude = jnp.exp(gain / (1.0 + fluence / SATURATION))
        turns = intensity * (KERR / (2.0 * math.pi))
        turns = turns - jnp.round(turns)
        square = turns * turns
        sin_kerr = turns * horner(SIN_TERMS, square)
        cos_kerr = horner(COS_TERMS, square)
        at = pl.ds(pl.multiple_of(step * block, block), block)
        kerr[at, :N] = (amplitude * (real * cos_kerr - imag * sin_kerr)).astype(BF16)
        kerr[at, N:] = (amplitude * (real * sin_kerr + imag * cos_kerr)).astype(BF16)

    loads[1].wait()

    def time_forward(part):
        @pl.loop(0, ROWS // 2)
        def _(pair):
            at = pl.ds(pl.multiple_of(pair * 2 * COLS, 2 * COLS), 2 * COLS)
            spectrum = lax.dot_general(
                forward[part * 2 * DEV : (part + 1) * 2 * DEV, :],
                kerr[at, :],
                (((1,), (1,)), ((), ())),
                preferred_element_type=F32,
            )
            for c in range(2):
                for r in range(2):
                    start = pl.multiple_of((c * ROWS + pair * 2 + r) * ROW_STRIDE, DEV)
                    spread[pl.ds(start, DEV), :] = spectrum[
                        c * DEV : (c + 1) * DEV, r * COLS : (r + 1) * COLS
                    ]

    def gather_tile(index):
        parts = [
            spread[pl.ds(c * ROWS * ROW_STRIDE + index, ROWS, stride=ROW_STRIDE), :] for c in range(2)
        ]
        return jnp.concatenate(parts, axis=0).astype(BF16)

    def send_spectrum(part):
        @pl.loop(1, DEV)
        def _(step):
            other = lax.rem(me + step, DEV)
            send1[part, other] = gather_tile(other)
            pltpu.make_async_remote_copy(
                src_ref=send1.at[part, other],
                dst_ref=recv1.at[part, place],
                send_sem=send_sem.at[part],
                recv_sem=recv_sem.at[part],
                device_id=(other // NARROW, lax.rem(other, NARROW)),
                device_id_type=MESH,
            ).start()

        recv1[part, place] = gather_tile(me)

    def make_circulant(part):
        half_phase = 0.5 * phase_ref[part * DEV + me]
        angle = jnp.full((1, N), half_phase, F32)
        cos_half = jnp.cos(angle)
        sin_half = jnp.sin(angle)
        real = jnp.concatenate([lines[part, j : j + 1, :] for j in range(4)], axis=1)
        imag = jnp.concatenate([lines[part, 4 + j : 5 + j, :] for j in range(4)], axis=1)
        turned = (real * cos_half - imag * sin_half, real * sin_half + imag * cos_half)
        for c in range(2):
            first = pltpu.roll(
                jnp.broadcast_to(turned[c], (COLS, N)), 0, 1, stride=1, stride_axis=0
            ).astype(BF16)
            for j in range(4):
                for k in range(4):
                    source = (k - j) % 4
                    circ[part, c, j * COLS : (j + 1) * COLS, k * COLS : (k + 1) * COLS] = first[
                        :, source * COLS : (source + 1) * COLS
                    ]

    def transform_plane(part):
        real_circ = circ[part, 0]
        imag_circ = circ[part, 1]
        group = 16

        @pl.loop(0, WIDE // group)
        def _(step):
            at = pl.multiple_of(step * group, group)
            lines_in = jnp.concatenate(
                [
                    recv1[part, pl.ds(j * WIDE + at, group)].reshape(group * 2 * ROWS, COLS)
                    for j in range(NARROW)
                ],
                axis=1,
            )
            by_real = jnp.dot(lines_in, real_circ, preferred_element_type=F32)
            by_imag = jnp.dot(lines_in, imag_circ, preferred_element_type=F32)
            by_real = by_real.reshape(group, 2, ROWS, N)
            by_imag = by_imag.reshape(group, 2, ROWS, N)
            rows = pl.ds(pl.multiple_of(step * group * ROWS, group * ROWS), group * ROWS)
            real = by_real[:, 0] - by_imag[:, 1]
            imag = by_imag[:, 0] + by_real[:, 1]
            plane[0, rows, :] = real.reshape(group * ROWS, N).astype(BF16)
            plane[1, rows, :] = imag.reshape(group * ROWS, N).astype(BF16)

        for half in range(2):
            cols = slice(half * 2 * COLS, (half + 1) * 2 * COLS)
            real_in = plane[0, :, cols]
            imag_in = plane[1, :, cols]
            real = jnp.dot(real_circ, real_in, preferred_element_type=F32) - jnp.dot(
                imag_circ, imag_in, preferred_element_type=F32
            )
            imag = jnp.dot(imag_circ, real_in, preferred_element_type=F32) + jnp.dot(
                real_circ, imag_in, preferred_element_type=F32
            )
            both = jnp.concatenate(
                [real.reshape(WIDE, ROWS, 2 * COLS), imag.reshape(WIDE, ROWS, 2 * COLS)], axis=1
            ).astype(BF16)
            for j in range(2):
                at = (2 * half + j) * WIDE
                send2[part, at : at + WIDE] = both[:, :, j * COLS : (j + 1) * COLS]

    def send_back(part):
        @pl.loop(1, DEV)
        def _(step):
            other = lax.rem(me + step, DEV)
            other_wide = other // NARROW
            other_narrow = lax.rem(other, NARROW)
            pltpu.make_async_remote_copy(
                src_ref=send2.at[part, other_narrow * WIDE + other_wide],
                dst_ref=recv2.at[part, me],
                send_sem=send_sem.at[2 + part],
                recv_sem=recv_sem.at[2 + part],
                device_id=(other_wide, other_narrow),
                device_id_type=MESH,
            ).start()

        recv2[part, me] = send2[part, place]

    def wait_bytes(buffer, part, sem):
        view = buffer.at[part, pl.ds(0, DEV - 1)]
        pltpu.make_async_copy(view, view, sem).wait()

    def time_inverse(part):
        @pl.loop(0, DEV, unroll=8)
        def _(index):
            tile = recv2[part, index].astype(F32)
            for c in range(2):
                spread[pl.ds(c * ROWS * ROW_STRIDE + index, ROWS, stride=ROW_STRIDE), :] = tile[
                    c * ROWS : (c + 1) * ROWS
                ]

        @pl.loop(0, ROWS // 2)
        def _(pair):
            columns = []
            for r in range(2):
                pieces = []
                for c in range(2):
                    start = pl.multiple_of((c * ROWS + pair * 2 + r) * ROW_STRIDE, DEV)
                    pieces.append(spread[pl.ds(start, DEV), :])
                columns.append(jnp.concatenate(pieces, axis=0))
            spectrum = jnp.concatenate(columns, axis=1).astype(BF16)
            result = lax.dot_general(
                spectrum,
                inverse[part * 2 * DEV : (part + 1) * 2 * DEV, :],
                (((0,), (0,)), ((), ())),
                preferred_element_type=F32,
            )
            at = pl.ds(pl.multiple_of(pair * 2 * COLS, 2 * COLS), 2 * COLS)
            if part == 0:
                total[at, :] = result
            else:
                result = result + total[at, :]
                for r in range(2):
                    for c in range(2):
                        out_ref[c, pair * 2 + r] = result[
                            r * COLS : (r + 1) * COLS, c * N : (c + 1) * N
                        ].astype(BF16)

    time_forward(0)
    pl.semaphore_wait(barrier, DEV - 1)
    send_spectrum(0)
    time_forward(1)
    send_spectrum(1)
    loads[2].wait()
    loads[3].wait()
    loads[4].wait()
    for part in range(2):
        make_circulant(part)
    for part in range(2):
        wait_bytes(recv1, part, recv_sem.at[part])
        transform_plane(part)
        send_back(part)
    for part in range(2):
        wait_bytes(recv2, part, recv_sem.at[2 + part])
        time_inverse(part)
    for part in range(2):
        wait_bytes(send1, part, send_sem.at[part])
        wait_bytes(send2, part, send_sem.at[2 + part])


def local(field, gain, spectral_phase):
    forward, inverse = time_tables()
    any_spec = pl.BlockSpec(memory_space=pl.ANY)
    return pl.pallas_call(
        kernel,
        out_shape=jax.ShapeDtypeStruct((2, ROWS, COLS, N), BF16),
        in_specs=[
            any_spec,
            pl.BlockSpec(memory_space=pltpu.VMEM),
            pl.BlockSpec(memory_space=pltpu.SMEM),
            any_spec,
            any_spec,
            any_spec,
        ],
        out_specs=pl.BlockSpec(memory_space=pltpu.VMEM),
        scratch_shapes=[
            pltpu.VMEM((2, ROWS, COLS, N), BF16),
            pltpu.VMEM((ROWS * COLS, 2 * N), BF16),
            pltpu.VMEM((2 * N, 2 * N), BF16),
            pltpu.VMEM((2 * N, 2 * N), BF16),
            pltpu.VMEM((2, 8, 128), F32),
            pltpu.VMEM((2, 2, N, N), BF16),
            pltpu.VMEM((COLS, ROWS), F32),
            pltpu.VMEM((2 * ROWS * ROW_STRIDE, COLS), F32),
            pltpu.VMEM((2, DEV, 2 * ROWS, COLS), BF16),
            pltpu.VMEM((2, DEV, 2 * ROWS, COLS), BF16),
            pltpu.VMEM((2, N, N), BF16),
            pltpu.VMEM((2, DEV, 2 * ROWS, COLS), BF16),
            pltpu.VMEM((2, DEV, 2 * ROWS, COLS), BF16),
            pltpu.VMEM((ROWS * COLS, 2 * N), F32),
            pltpu.SemaphoreType.DMA((5,)),
            pltpu.SemaphoreType.DMA((4,)),
            pltpu.SemaphoreType.DMA((4,)),
        ],
        compiler_params=pltpu.CompilerParams(
            collective_id=0, has_side_effects=True, vmem_limit_bytes=56 << 20
        ),
    )(
        field,
        gain,
        spectral_phase,
        jnp.asarray(forward),
        jnp.asarray(inverse),
        jnp.asarray(line_kernels()),
    )


def solution(mesh):
    in_specs = (P(None, "wide", "narrow", None), P("wide", "narrow"), P())
    out_specs = P(None, "wide", "narrow", None)
    return jax.shard_map(local, mesh=mesh, in_specs=in_specs, out_specs=out_specs, check_vma=False)
```

profile of v0, /device:TPU:9, one launch (start us, length us, event | category | flops | bytes accessed | tf_op | source)
XLA Modules:
  0.0 124.6 jit_solution(152010366562735496)
XLA Ops:
  0.0 121.5 %shard_map.64 = bf16[2,8,128,512]{3,2,1,0:T(8,128)(2,1)} custom-call(bf16[2,8,128,512]{3,2,1,0:T(8,128)(2,1)} %field_hbm.1, f32[8,128]{1,0:T(8,128)} %gain_ref.1, f32[512]{0:T(512)} %phase_ref.1, bf16[1024,1024]{1,0:T(8,128)(2,1)} %constant.4.clone.forward_hbm.inverse_hbm, bf16[1024,1024]{1,0:T(8,128)(2,1)} %constant.4.clone.forward_hbm.inverse_hbm, ...), custom_call_target="tpu_custom_call" | custom-call | tf_op jit(solution)/shard_map/pallas_call | solution.py:330
  121.5 3.1 %copy.8 = bf16[2,8,128,512]{3,2,1,0:T(8,128)(2,1)} copy(bf16[2,8,128,512]{3,2,1,0:T(8,128)(2,1)} %shard_map.64) | data formatting | bytes 4194304
where the time goes:
time: 125 us
  Pallas kernels  121 us (97%)
  local copies, waits for them, and re-layouts  3.1 us (2%)
    pallas_call x1, Pallas kernels, local(): pl.pallas_call(kernel, out_shape=jax.ShapeDtypeStruct((2, ROWS, COLS, N),...  121 us
    unnamed x1, local copies, waits for them, and re-layouts  3.1 us

commit v1 on v0

--- a/solution.py
+++ b/solution.py
@@ -14,6 +14,7 @@
 
 N = 512
 DEV = 256
+HALF = N // 2
 WIDE = 64
 NARROW = 4
 ROWS = 8
@@ -21,7 +22,7 @@
 KERR = 0.25
 SATURATION = 1.0
 DIFFRACT = 120.0
-ROW_STRIDE = DEV
+ROW_STRIDE = DEV + 8
 
 def _fit(func, count):
     nodes = 0.125 * (1.0 - np.cos((np.arange(400) + 0.5) * np.pi / 400))
@@ -29,8 +30,8 @@
     return [float(v) for v in np.linalg.lstsq(powers, func(np.sqrt(nodes)), rcond=None)[0]]
 
 
-SIN_TERMS = _fit(lambda z: np.sin(2 * np.pi * z) / z, 7)
-COS_TERMS = _fit(lambda z: np.cos(2 * np.pi * z), 7)
+SIN_TERMS = _fit(lambda z: np.sin(2 * np.pi * z) / z, 6)
+COS_TERMS = _fit(lambda z: np.cos(2 * np.pi * z), 6)
 
 
 def horner(terms, value):
@@ -53,10 +54,12 @@
 
 def time_tables():
     cos_table, sin_table = dft_tables(N)
-    forward = np.block([[cos_table, sin_table], [-sin_table, cos_table]])
-    inverse = np.block([[cos_table, sin_table], [-sin_table, cos_table]])
-    order = np.arange(2 * N).reshape(2, 2, DEV).transpose(1, 0, 2).reshape(-1)
-    return forward[order].astype(BF16), inverse[order].astype(BF16)
+    tables = []
+    for part in range(2):
+        cos_part = cos_table[part::2, :HALF]
+        sin_part = sin_table[part::2, :HALF]
+        tables.append(np.block([[cos_part, sin_part], [-sin_part, cos_part]]))
+    return np.stack(tables).astype(BF16)
 
 
 def line_kernels():
@@ -71,14 +74,13 @@
     field_hbm,
     gain_ref,
     phase_ref,
-    forward_hbm,
-    inverse_hbm,
+    table_hbm,
     lines_hbm,
-    out_ref,
+    real_hbm,
+    imag_hbm,
     field,
     kerr,
-    forward,
-    inverse,
+    table,
     lines,
     circ,
     gain_t,
@@ -92,6 +94,7 @@
     load_sem,
     send_sem,
     recv_sem,
+    store_sem,
 ):
     wide = lax.axis_index("wide")
     narrow = lax.axis_index("narrow")
@@ -99,6 +102,17 @@
     place = narrow * WIDE + wide
 
     barrier = pltpu.get_barrier_semaphore()
+
+    fields = []
+    for pair in range(ROWS // 2):
+        at = pl.ds(2 * pair, 2)
+        fields.append(pltpu.make_async_copy(field_hbm.at[:, at], field.at[:, at], load_sem.at[pair]))
+    loads = [
+        pltpu.make_async_copy(table_hbm, table, load_sem.at[4]),
+        pltpu.make_async_copy(lines_hbm.at[pl.ds(2 * me, 2)], lines, load_sem.at[5]),
+    ]
+    for load in fields + loads:
+        load.start()
 
     @pl.loop(1, DEV)
     def _(step):
@@ -107,60 +121,47 @@
             barrier, inc=1, device_id=(other // NARROW, lax.rem(other, NARROW)), device_id_type=MESH
         )
 
-    loads = [
-        pltpu.make_async_copy(field_hbm, field, load_sem.at[0]),
-        pltpu.make_async_copy(forward_hbm, forward, load_sem.at[1]),
-        pltpu.make_async_copy(lines_hbm.at[pl.ds(me, 1)], lines.at[pl.ds(0, 1)], load_sem.at[2]),
-        pltpu.make_async_copy(lines_hbm.at[pl.ds(DEV + me, 1)], lines.at[pl.ds(1, 1)], load_sem.at[3]),
-        pltpu.make_async_copy(inverse_hbm, inverse, load_sem.at[4]),
-    ]
-    for load in loads:
-        load.start()
-
     gain_t[...] = jnp.transpose(gain_ref[...])
-    loads[0].wait()
-
     block = 32
 
-    @pl.loop(0, ROWS * COLS // block)
-    def _(step):
-        row = step // (COLS // block)
-        col = pl.multiple_of(lax.rem(step, COLS // block) * block, block)
-        real = field[0, row, pl.ds(col, block), :].astype(F32)
-        imag = field[1, row, pl.ds(col, block), :].astype(F32)
-        intensity = real * real + imag * imag
-        fluence = jnp.sum(intensity, axis=1, keepdims=True) * (1.0 / N)
-        gains = gain_t[pl.ds(col, block), :]
-        lane = lax.broadcasted_iota(jnp.int32, gains.shape, 1)
-        gain = jnp.sum(jnp.where(lane == row, gains, 0.0), axis=1, keepdims=True)
-        amplitude = jnp.exp(gain / (1.0 + fluence / SATURATION))
-        turns = intensity * (KERR / (2.0 * math.pi))
-        turns = turns - jnp.round(turns)
-        square = turns * turns
-        sin_kerr = turns * horner(SIN_TERMS, square)
-        cos_kerr = horner(COS_TERMS, square)
-        at = pl.ds(pl.multiple_of(step * block, block), block)
-        kerr[at, :N] = (amplitude * (real * cos_kerr - imag * sin_kerr)).astype(BF16)
-        kerr[at, N:] = (amplitude * (real * sin_kerr + imag * cos_kerr)).astype(BF16)
-
-    loads[1].wait()
-
-    def time_forward(part):
-        @pl.loop(0, ROWS // 2)
-        def _(pair):
-            at = pl.ds(pl.multiple_of(pair * 2 * COLS, 2 * COLS), 2 * COLS)
-            spectrum = lax.dot_general(
-                forward[part * 2 * DEV : (part + 1) * 2 * DEV, :],
-                kerr[at, :],
-                (((1,), (1,)), ((), ())),
-                preferred_element_type=F32,
-            )
-            for c in range(2):
-                for r in range(2):
-                    start = pl.multiple_of((c * ROWS + pair * 2 + r) * ROW_STRIDE, DEV)
-                    spread[pl.ds(start, DEV), :] = spectrum[
-                        c * DEV : (c + 1) * DEV, r * COLS : (r + 1) * COLS
-                    ]
+    def kerr_pair(pair):
+        @pl.loop(0, 2 * COLS // block)
+        def _(step):
+            row = 2 * pair + step // (COLS // block)
+            col = pl.multiple_of(lax.rem(step, COLS // block) * block, block)
+            real = field[0, row, pl.ds(col, block), :].astype(F32)
+            imag = field[1, row, pl.ds(col, block), :].astype(F32)
+            intensity = real * real + imag * imag
+            fluence = jnp.sum(intensity, axis=1, keepdims=True) * (1.0 / N)
+            gains = gain_t[pl.ds(col, block), :]
+            lane = lax.broadcasted_iota(jnp.int32, gains.shape, 1)
+            gain = jnp.sum(jnp.where(lane == row, gains, 0.0), axis=1, keepdims=True)
+            amplitude = jnp.exp(gain / (1.0 + fluence / SATURATION))
+            turns = intensity * (KERR / (2.0 * math.pi))
+            turns = turns - jnp.round(turns)
+            square = turns * turns
+            sin_kerr = amplitude * turns * horner(SIN_TERMS, square)
+            cos_kerr = amplitude * horner(COS_TERMS, square)
+            kerr_real = real * cos_kerr - imag * sin_kerr
+            kerr_imag = real * sin_kerr + imag * cos_kerr
+            at = pl.ds(pl.multiple_of(pair * 2 * COLS + step * block, block), block)
+            for c, value in enumerate((kerr_real, kerr_imag)):
+                first = value[:, :HALF]
+                second = value[:, HALF:]
+                kerr[0, at, c * HALF : (c + 1) * HALF] = (first + second).astype(BF16)
+                kerr[1, at, c * HALF : (c + 1) * HALF] = (first - second).astype(BF16)
+
+    def time_forward(part, pair):
+        at = pl.ds(pl.multiple_of(pair * 2 * COLS, 2 * COLS), 2 * COLS)
+        spectrum = lax.dot_general(
+            table[part], kerr[part, at, :], (((1,), (1,)), ((), ())), preferred_element_type=F32
+        )
+        for c in range(2):
+            for r in range(2):
+                start = pl.multiple_of((c * ROWS + pair * 2 + r) * ROW_STRIDE, 8)
+                spread[pl.ds(start, DEV), :] = spectrum[
+                    c * DEV : (c + 1) * DEV, r * COLS : (r + 1) * COLS
+                ]
 
     def gather_tile(index):
         parts = [
@@ -185,7 +186,7 @@
         recv1[part, place] = gather_tile(me)
 
     def make_circulant(part):
-        half_phase = 0.5 * phase_ref[part * DEV + me]
+        half_phase = 0.5 * phase_ref[2 * me + part]
         angle = jnp.full((1, N), half_phase, F32)
         cos_half = jnp.cos(angle)
         sin_half = jnp.sin(angle)
@@ -266,6 +267,13 @@
         view = buffer.at[part, pl.ds(0, DEV - 1)]
         pltpu.make_async_copy(view, view, sem).wait()
 
+    def stores(pair):
+        at = pl.ds(pair * 2, 2)
+        return [
+            pltpu.make_async_copy(field.at[c, at], out.at[at], store_sem.at[pair, c])
+            for c, out in enumerate((real_hbm, imag_hbm))
+        ]
+
     def time_inverse(part):
         @pl.loop(0, DEV, unroll=8)
         def _(index):
@@ -281,13 +289,13 @@
             for r in range(2):
                 pieces = []
                 for c in range(2):
-                    start = pl.multiple_of((c * ROWS + pair * 2 + r) * ROW_STRIDE, DEV)
+                    start = pl.multiple_of((c * ROWS + pair * 2 + r) * ROW_STRIDE, 8)
                     pieces.append(spread[pl.ds(start, DEV), :])
                 columns.append(jnp.concatenate(pieces, axis=0))
             spectrum = jnp.concatenate(columns, axis=1).astype(BF16)
             result = lax.dot_general(
                 spectrum,
-                inverse[part * 2 * DEV : (part + 1) * 2 * DEV, :],
+                table[part],
                 (((0,), (0,)), ((), ())),
                 preferred_element_type=F32,
             )
@@ -295,21 +303,33 @@
             if part == 0:
                 total[at, :] = result
             else:
-                result = result + total[at, :]
-                for r in range(2):
-                    for c in range(2):
-                        out_ref[c, pair * 2 + r] = result[
-                            r * COLS : (r + 1) * COLS, c * N : (c + 1) * N
-                        ].astype(BF16)
-
-    time_forward(0)
+                even = total[at, :]
+                for half, value in enumerate((even + result, even - result)):
+                    value = value.astype(BF16)
+                    for r in range(2):
+                        for c in range(2):
+                            field[c, pair * 2 + r, :, half * HALF : (half + 1) * HALF] = value[
+                                r * COLS : (r + 1) * COLS, c * HALF : (c + 1) * HALF
+                            ]
+                for store in stores(pair):
+                    store.start()
+
+    for pair in range(ROWS // 2):
+        fields[pair].wait()
+        kerr_pair(pair)
+        if pair == 0:
+            loads[0].wait()
+        time_forward(0, pair)
+
     pl.semaphore_wait(barrier, DEV - 1)
     send_spectrum(0)
-    time_forward(1)
+
+    @pl.loop(0, ROWS // 2)
+    def _(pair):
+        time_forward(1, pair)
+
     send_spectrum(1)
-    loads[2].wait()
-    loads[3].wait()
-    loads[4].wait()
+    loads[1].wait()
     for part in range(2):
         make_circulant(part)
     for part in range(2):
@@ -319,31 +339,50 @@
     for part in range(2):
         wait_bytes(recv2, part, recv_sem.at[2 + part])
         time_inverse(part)
+    for pair in range(ROWS // 2):
+        for store in stores(pair):
+            store.wait()
     for part in range(2):
         wait_bytes(send1, part, send_sem.at[part])
         wait_bytes(send2, part, send_sem.at[2 + part])
 
 
+def gather_parts(real_hbm, imag_hbm, out_hbm, held, load_sem, store_sem):
+    pieces = [(c, row) for row in range(ROWS) for c in range(2)]
+    loads = [
+        pltpu.make_async_copy((real_hbm, imag_hbm)[c].at[row], held.at[c, row], load_sem.at[c, row])
+        for c, row in pieces
+    ]
+    stores = [
+        pltpu.make_async_copy(held.at[c, row], out_hbm.at[c, row], store_sem.at[c, row])
+        for c, row in pieces
+    ]
+    for load in loads:
+        load.start()
+    for load, store in zip(loads, stores):
+        load.wait()
+        store.start()
+    for store in stores:
+        store.wait()
+
+
 def local(field, gain, spectral_phase):
-    forward, inverse = time_tables()
-    any_spec = pl.BlockSpec(memory_space=pl.ANY)
-    return pl.pallas_call(
+    hbm_spec = pl.BlockSpec(memory_space=pltpu.HBM)
+    real, imag = pl.pallas_call(
         kernel,
-        out_shape=jax.ShapeDtypeStruct((2, ROWS, COLS, N), BF16),
+        out_shape=[jax.ShapeDtypeStruct((ROWS, COLS, N), BF16)] * 2,
         in_specs=[
-            any_spec,
+            hbm_spec,
             pl.BlockSpec(memory_space=pltpu.VMEM),
             pl.BlockSpec(memory_space=pltpu.SMEM),
-            any_spec,
-            any_spec,
-            any_spec,
+            hbm_spec,
+            hbm_spec,
         ],
-        out_specs=pl.BlockSpec(memory_space=pltpu.VMEM),
+        out_specs=[hbm_spec] * 2,
         scratch_shapes=[
             pltpu.VMEM((2, ROWS, COLS, N), BF16),
-            pltpu.VMEM((ROWS * COLS, 2 * N), BF16),
-            pltpu.VMEM((2 * N, 2 * N), BF16),
-            pltpu.VMEM((2 * N, 2 * N), BF16),
+            pltpu.VMEM((2, ROWS * COLS, N), BF16),
+            pltpu.VMEM((2, N, N), BF16),
             pltpu.VMEM((2, 8, 128), F32),
             pltpu.VMEM((2, 2, N, N), BF16),
             pltpu.VMEM((COLS, ROWS), F32),
@@ -353,10 +392,11 @@
             pltpu.VMEM((2, N, N), BF16),
             pltpu.VMEM((2, DEV, 2 * ROWS, COLS), BF16),
             pltpu.VMEM((2, DEV, 2 * ROWS, COLS), BF16),
-            pltpu.VMEM((ROWS * COLS, 2 * N), F32),
-            pltpu.SemaphoreType.DMA((5,)),
+            pltpu.VMEM((ROWS * COLS, N), F32),
+            pltpu.SemaphoreType.DMA((6,)),
             pltpu.SemaphoreType.DMA((4,)),
             pltpu.SemaphoreType.DMA((4,)),
+            pltpu.SemaphoreType.DMA((ROWS // 2, 2)),
         ],
         compiler_params=pltpu.CompilerParams(
             collective_id=0, has_side_effects=True, vmem_limit_bytes=56 << 20
@@ -365,10 +405,21 @@
         field,
         gain,
         spectral_phase,
-        jnp.asarray(forward),
-        jnp.asarray(inverse),
+        jnp.asarray(time_tables()),
         jnp.asarray(line_kernels()),
     )
+    return pl.pallas_call(
+        gather_parts,
+        out_shape=jax.ShapeDtypeStruct((2, ROWS, COLS, N), BF16),
+        in_specs=[hbm_spec] * 2,
+        out_specs=hbm_spec,
+        scratch_shapes=[
+            pltpu.VMEM((2, ROWS, COLS, N), BF16),
+            pltpu.SemaphoreType.DMA((2, ROWS)),
+            pltpu.SemaphoreType.DMA((2, ROWS)),
+        ],
+        compiler_params=pltpu.CompilerParams(vmem_limit_bytes=56 << 20),
+    )(real, imag)
 
 
 def solution(mesh):

time: 125 us -> 120 us (0.960)
  local copies, waits for them, and re-layouts: 3.1 us -> 0 us
    unnamed x1 -> x0, local copies, waits for them, and re-layouts: 3.1 us -> none
    pallas_call x1 -> x2, Pallas kernels: 121 us -> 120 us  [the longest x1 117 us: local(): pl.pallas_call(kernel, out_shape=[jax.ShapeDtypeStruct((ROWS, COLS, N), B...]
where the time goes in v1:
time: 120 us
  Pallas kernels  120 us (100%)
    pallas_call x1, Pallas kernels, local(): pl.pallas_call(kernel, out_shape=[jax.ShapeDtypeStruct((ROWS, COLS, N), B...  117 us
    pallas_call x1, Pallas kernels, local(): pl.pallas_call(gather_parts, out_shape=jax.ShapeDtypeStruct((2, ROWS, COL...  2.57 us

profile of v1, /device:TPU:9, one launch (start us, length us, event | category | flops | bytes accessed | tf_op | source)
XLA Modules:
  0.0 119.6 jit_solution(13679089908632394959)
XLA Ops:
  0.0 117.0 %shard_map.55 = (bf16[8,128,512]{2,1,0:T(8,128)(2,1)}, bf16[8,128,512]{2,1,0:T(8,128)(2,1)}) custom-call(bf16[2,8,128,512]{3,2,1,0:T(8,128)(2,1)} %field_hbm.1, f32[8,128]{1,0:T(8,128)} %gain_ref.1, f32[512]{0:T(512)} %phase_ref.1, bf16[2,512,512]{2,1,0:T(8,128)(2,1)} %constant.4.clone.table_hbm, f32[512,8,128]{2,1,0:T(8,128)} %constant.5.clone.lines_hbm), custom_call_target="tpu_custom_call" | custom-call | tf_op jit(solution)/shard_map/pallas_call | solution.py:371
  117.0 2.6 %shard_map.56 = bf16[2,8,128,512]{3,2,1,0:T(8,128)(2,1)} custom-call(bf16[8,128,512]{2,1,0:T(8,128)(2,1)} %get-tuple-element.7.real_hbm, bf16[8,128,512]{2,1,0:T(8,128)(2,1)} %get-tuple-element.8.imag_hbm), custom_call_target="tpu_custom_call" | custom-call | tf_op jit(solution)/shard_map/pallas_call | solution.py:411

commit v2 on v1

--- a/solution.py
+++ b/solution.py
@@ -22,6 +22,7 @@
 KERR = 0.25
 SATURATION = 1.0
 DIFFRACT = 120.0
+SEND_UNROLL = 1
 ROW_STRIDE = DEV + 8
 
 def _fit(func, count):
@@ -72,8 +73,8 @@
 
 def kernel(
     field_hbm,
-    gain_ref,
-    phase_ref,
+    gain_hbm,
+    phase_hbm,
     table_hbm,
     lines_hbm,
     real_hbm,
@@ -83,6 +84,8 @@
     table,
     lines,
     circ,
+    gain_ref,
+    phase_ref,
     gain_t,
     spread,
     send1,
@@ -90,7 +93,8 @@
     plane,
     send2,
     recv2,
-    total,
+    even,
+    odd,
     load_sem,
     send_sem,
     recv_sem,
@@ -109,9 +113,11 @@
         fields.append(pltpu.make_async_copy(field_hbm.at[:, at], field.at[:, at], load_sem.at[pair]))
     loads = [
         pltpu.make_async_copy(table_hbm, table, load_sem.at[4]),
-        pltpu.make_async_copy(lines_hbm.at[pl.ds(2 * me, 2)], lines, load_sem.at[5]),
+        pltpu.make_async_copy(lines_hbm.at[pl.ds(2 * place, 2)], lines, load_sem.at[5]),
+        pltpu.make_async_copy(phase_hbm, phase_ref, load_sem.at[7]),
     ]
-    for load in fields + loads:
+    load_gain = pltpu.make_async_copy(gain_hbm, gain_ref, load_sem.at[6])
+    for load in [load_gain] + fields + loads:
         load.start()
 
     @pl.loop(1, DEV)
@@ -121,11 +127,12 @@
             barrier, inc=1, device_id=(other // NARROW, lax.rem(other, NARROW)), device_id_type=MESH
         )
 
+    load_gain.wait()
     gain_t[...] = jnp.transpose(gain_ref[...])
     block = 32
 
     def kerr_pair(pair):
-        @pl.loop(0, 2 * COLS // block)
+        @pl.loop(0, 2 * COLS // block, unroll=4)
         def _(step):
             row = 2 * pair + step // (COLS // block)
             col = pl.multiple_of(lax.rem(step, COLS // block) * block, block)
@@ -151,8 +158,11 @@
                 kerr[0, at, c * HALF : (c + 1) * HALF] = (first + second).astype(BF16)
                 kerr[1, at, c * HALF : (c + 1) * HALF] = (first - second).astype(BF16)
 
+    def pair_rows(pair):
+        return pl.ds(pl.multiple_of(pair * 2 * COLS, 2 * COLS), 2 * COLS)
+
     def time_forward(part, pair):
-        at = pl.ds(pl.multiple_of(pair * 2 * COLS, 2 * COLS), 2 * COLS)
+        at = pair_rows(pair)
         spectrum = lax.dot_general(
             table[part], kerr[part, at, :], (((1,), (1,)), ((), ())), preferred_element_type=F32
         )
@@ -169,24 +179,43 @@
         ]
         return jnp.concatenate(parts, axis=0).astype(BF16)
 
+    def partner(step):
+        other_wide = lax.rem(wide + step, WIDE)
+        turn = step // WIDE
+        other_chip = lax.rem(narrow // 2 + turn // 2, 2)
+        other_core = lax.rem(narrow + turn, 2)
+        other_narrow = other_chip * 2 + other_core
+        return other_wide, other_narrow, other_narrow * WIDE + other_wide
+
+    def partner_low_first(step):
+        turn = lax.rem(step, WIDE)
+        core_turn, turn = turn // 32, lax.rem(turn, 32)
+        z_turn, turn = turn // 8, lax.rem(turn, 8)
+        other_x = lax.rem(wide // 32 + turn // 4, 2)
+        other_z = lax.rem(wide // 4 + z_turn, 4) + step // WIDE * 4
+        other_y = lax.rem(wide + turn, 4)
+        other_wide = other_x * 32 + other_z * 4 + other_y
+        other_narrow = lax.rem(narrow // 2 + 1, 2) * 2 + lax.rem(narrow + core_turn, 2)
+        return other_wide, other_narrow, other_narrow * WIDE + other_wide
+
     def send_spectrum(part):
-        @pl.loop(1, DEV)
+        @pl.loop(1, DEV, unroll=SEND_UNROLL)
         def _(step):
-            other = lax.rem(me + step, DEV)
+            other_wide, other_narrow, other = partner(step)
             send1[part, other] = gather_tile(other)
             pltpu.make_async_remote_copy(
                 src_ref=send1.at[part, other],
                 dst_ref=recv1.at[part, place],
                 send_sem=send_sem.at[part],
                 recv_sem=recv_sem.at[part],
-                device_id=(other // NARROW, lax.rem(other, NARROW)),
+                device_id=(other_wide, other_narrow),
                 device_id_type=MESH,
             ).start()
 
-        recv1[part, place] = gather_tile(me)
+        recv1[part, place] = gather_tile(place)
 
     def make_circulant(part):
-        half_phase = 0.5 * phase_ref[2 * me + part]
+        half_phase = 0.5 * phase_ref[2 * place + part]
         angle = jnp.full((1, N), half_phase, F32)
         cos_half = jnp.cos(angle)
         sin_half = jnp.sin(angle)
@@ -247,24 +276,27 @@
                 send2[part, at : at + WIDE] = both[:, :, j * COLS : (j + 1) * COLS]
 
     def send_back(part):
-        @pl.loop(1, DEV)
-        def _(step):
-            other = lax.rem(me + step, DEV)
-            other_wide = other // NARROW
-            other_narrow = lax.rem(other, NARROW)
-            pltpu.make_async_remote_copy(
-                src_ref=send2.at[part, other_narrow * WIDE + other_wide],
-                dst_ref=recv2.at[part, me],
-                send_sem=send_sem.at[2 + part],
-                recv_sem=recv_sem.at[2 + part],
-                device_id=(other_wide, other_narrow),
-                device_id_type=MESH,
-            ).start()
-
-        recv2[part, me] = send2[part, place]
-
-    def wait_bytes(buffer, part, sem):
-        view = buffer.at[part, pl.ds(0, DEV - 1)]
+        for half in range(2):
+
+            @pl.loop(max(1, half * DEV // 2), (half + 1) * DEV // 2, unroll=SEND_UNROLL)
+            def _(step):
+                if part == 1 and half == 1:
+                    other_wide, other_narrow, other = partner_low_first(step - DEV // 2)
+                else:
+                    other_wide, other_narrow, other = partner(step)
+                pltpu.make_async_remote_copy(
+                    src_ref=send2.at[part, other],
+                    dst_ref=recv2.at[part, place],
+                    send_sem=send_sem.at[2 + part],
+                    recv_sem=recv_sem.at[2 + 2 * part + half],
+                    device_id=(other_wide, other_narrow),
+                    device_id_type=MESH,
+                ).start()
+
+        recv2[part, place] = send2[part, place]
+
+    def wait_bytes(buffer, part, sem, count=DEV - 1):
+        view = buffer.at[part, pl.ds(0, count)]
         pltpu.make_async_copy(view, view, sem).wait()
 
     def stores(pair):
@@ -274,45 +306,62 @@
             for c, out in enumerate((real_hbm, imag_hbm))
         ]
 
-    def time_inverse(part):
-        @pl.loop(0, DEV, unroll=8)
-        def _(index):
+    def unpack(part, start, count):
+        @pl.loop(0, count, unroll=8)
+        def _(step):
+            index = start + step
             tile = recv2[part, index].astype(F32)
             for c in range(2):
                 spread[pl.ds(c * ROWS * ROW_STRIDE + index, ROWS, stride=ROW_STRIDE), :] = tile[
                     c * ROWS : (c + 1) * ROWS
                 ]
 
+    def time_inverse(part, pair, start, count):
+        columns = []
+        for r in range(2):
+            pieces = []
+            for c in range(2):
+                base = pl.multiple_of((c * ROWS + pair * 2 + r) * ROW_STRIDE + start, 8)
+                pieces.append(spread[pl.ds(base, count), :])
+            columns.append(jnp.concatenate(pieces, axis=0))
+        spectrum = jnp.concatenate(columns, axis=1).astype(BF16)
+        rows = [table[part, pl.ds(pl.multiple_of(c * DEV + start, WIDE), count), :] for c in range(2)]
+        return lax.dot_general(
+            spectrum,
+            jnp.concatenate(rows, axis=0),
+            (((0,), (0,)), ((), ())),
+            preferred_element_type=F32,
+        )
+
+    def inverse_even():
+        unpack(0, 0, DEV)
+
         @pl.loop(0, ROWS // 2)
         def _(pair):
-            columns = []
-            for r in range(2):
-                pieces = []
-                for c in range(2):
-                    start = pl.multiple_of((c * ROWS + pair * 2 + r) * ROW_STRIDE, 8)
-                    pieces.append(spread[pl.ds(start, DEV), :])
-                columns.append(jnp.concatenate(pieces, axis=0))
-            spectrum = jnp.concatenate(columns, axis=1).astype(BF16)
-            result = lax.dot_general(
-                spectrum,
-                table[part],
-                (((0,), (0,)), ((), ())),
-                preferred_element_type=F32,
-            )
-            at = pl.ds(pl.multiple_of(pair * 2 * COLS, 2 * COLS), 2 * COLS)
-            if part == 0:
-                total[at, :] = result
-            else:
-                even = total[at, :]
-                for half, value in enumerate((even + result, even - result)):
-                    value = value.astype(BF16)
-                    for r in range(2):
-                        for c in range(2):
-                            field[c, pair * 2 + r, :, half * HALF : (half + 1) * HALF] = value[
-                                r * COLS : (r + 1) * COLS, c * HALF : (c + 1) * HALF
-                            ]
-                for store in stores(pair):
-                    store.start()
+            even[pair_rows(pair), :] = time_inverse(0, pair, 0, DEV)
+
+    def inverse_odd(half):
+        start = pl.multiple_of(lax.rem(narrow // 2 + half, 2) * 2 * WIDE, 2 * WIDE)
+        unpack(1, start, 2 * WIDE)
+
+        @pl.loop(0, ROWS // 2)
+        def _(pair):
+            at = pair_rows(pair)
+            result = time_inverse(1, pair, start, 2 * WIDE)
+            if half == 0:
+                odd[at, :] = result
+                return
+            result = result + odd[at, :]
+            first = even[at, :]
+            for j, value in enumerate((first + result, first - result)):
+                value = value.astype(BF16)
+                for r in range(2):
+                    for c in range(2):
+                        field[c, pair * 2 + r, :, j * HALF : (j + 1) * HALF] = value[
+                            r * COLS : (r + 1) * COLS, c * HALF : (c + 1) * HALF
+                        ]
+            for store in stores(pair):
+                store.start()
 
     for pair in range(ROWS // 2):
         fields[pair].wait()
@@ -330,15 +379,20 @@
 
     send_spectrum(1)
     loads[1].wait()
+    loads[2].wait()
     for part in range(2):
         make_circulant(part)
     for part in range(2):
         wait_bytes(recv1, part, recv_sem.at[part])
         transform_plane(part)
         send_back(part)
-    for part in range(2):
-        wait_bytes(recv2, part, recv_sem.at[2 + part])
-        time_inverse(part)
+    wait_bytes(recv2, 0, recv_sem.at[2], DEV // 2 - 1)
+    wait_bytes(recv2, 0, recv_sem.at[3], DEV // 2)
+    inverse_even()
+    wait_bytes(recv2, 1, recv_sem.at[4], DEV // 2 - 1)
+    inverse_odd(0)
+    wait_bytes(recv2, 1, recv_sem.at[5], DEV // 2)
+    inverse_odd(1)
     for pair in range(ROWS // 2):
         for store in stores(pair):
             store.wait()
@@ -373,8 +427,8 @@
         out_shape=[jax.ShapeDtypeStruct((ROWS, COLS, N), BF16)] * 2,
         in_specs=[
             hbm_spec,
-            pl.BlockSpec(memory_space=pltpu.VMEM),
-            pl.BlockSpec(memory_space=pltpu.SMEM),
+            hbm_spec,
+            hbm_spec,
             hbm_spec,
             hbm_spec,
         ],
@@ -385,6 +439,8 @@
             pltpu.VMEM((2, N, N), BF16),
             pltpu.VMEM((2, 8, 128), F32),
             pltpu.VMEM((2, 2, N, N), BF16),
+            pltpu.VMEM((ROWS, COLS), F32),
+            pltpu.SMEM((N,), F32),
             pltpu.VMEM((COLS, ROWS), F32),
             pltpu.VMEM((2 * ROWS * ROW_STRIDE, COLS), F32),
             pltpu.VMEM((2, DEV, 2 * ROWS, COLS), BF16),
@@ -393,9 +449,10 @@
             pltpu.VMEM((2, DEV, 2 * ROWS, COLS), BF16),
             pltpu.VMEM((2, DEV, 2 * ROWS, COLS), BF16),
             pltpu.VMEM((ROWS * COLS, N), F32),
+            pltpu.VMEM((ROWS * COLS, N), F32),
+            pltpu.SemaphoreType.DMA((8,)),
+            pltpu.SemaphoreType.DMA((4,)),
             pltpu.SemaphoreType.DMA((6,)),
-            pltpu.SemaphoreType.DMA((4,)),
-            pltpu.SemaphoreType.DMA((4,)),
             pltpu.SemaphoreType.DMA((ROWS // 2, 2)),
         ],
         compiler_params=pltpu.CompilerParams(

time: 120 us -> 117 us (0.975); the launches traced: 120 us -> 115 us
  Pallas kernels: 120 us -> 115 us
    pallas_call x1, Pallas kernels: 117 us -> 112 us  [local(): pl.pallas_call(kernel, out_shape=[jax.ShapeDtypeStruct((ROWS, COLS, N), B...]
where the time goes in v2:
time: 117 us; the launch traced here: 115 us
  Pallas kernels  115 us (98%)
    pallas_call x1, Pallas kernels, local(): pl.pallas_call(kernel, out_shape=[jax.ShapeDtypeStruct((ROWS, COLS, N), B...  112 us
    pallas_call x1, Pallas kernels, local(): pl.pallas_call(gather_parts, out_shape=jax.ShapeDtypeStruct((2, ROWS, COL...  2.57 us

profile of v2, /device:TPU:9, one launch (start us, length us, event | category | flops | bytes accessed | tf_op | source)
XLA Modules:
  0.0 114.8 jit_solution(13090378783389729523)
XLA Ops:
  0.0 112.3 %shard_map.55 = (bf16[8,128,512]{2,1,0:T(8,128)(2,1)}, bf16[8,128,512]{2,1,0:T(8,128)(2,1)}) custom-call(bf16[2,8,128,512]{3,2,1,0:T(8,128)(2,1)} %field_hbm.1, f32[8,128]{1,0:T(8,128)} %gain_hbm.1, f32[512]{0:T(512)} %phase_hbm.1, bf16[2,512,512]{2,1,0:T(8,128)(2,1)} %constant.4.clone.table_hbm, f32[512,8,128]{2,1,0:T(8,128)} %constant.5.clone.lines_hbm), custom_call_target="tpu_custom_call" | custom-call | tf_op jit(solution)/shard_map/pallas_call | solution.py:425
  112.3 2.6 %shard_map.56 = bf16[2,8,128,512]{3,2,1,0:T(8,128)(2,1)} custom-call(bf16[8,128,512]{2,1,0:T(8,128)(2,1)} %get-tuple-element.7.real_hbm, bf16[8,128,512]{2,1,0:T(8,128)(2,1)} %get-tuple-element.8.imag_hbm), custom_call_target="tpu_custom_call" | custom-call | tf_op jit(solution)/shard_map/pallas_call | solution.py:468

commit v3 on v2

--- a/solution.py
+++ b/solution.py
@@ -189,11 +189,11 @@
 
     def partner_low_first(step):
         turn = lax.rem(step, WIDE)
-        core_turn, turn = turn // 32, lax.rem(turn, 32)
-        z_turn, turn = turn // 8, lax.rem(turn, 8)
-        other_x = lax.rem(wide // 32 + turn // 4, 2)
+        other_y, turn = turn // 16, lax.rem(turn, 16)
+        z_turn, turn = turn // 4, lax.rem(turn, 4)
+        core_turn = turn // 2
+        other_x = lax.rem(wide // 32 + turn, 2)
         other_z = lax.rem(wide // 4 + z_turn, 4) + step // WIDE * 4
-        other_y = lax.rem(wide + turn, 4)
         other_wide = other_x * 32 + other_z * 4 + other_y
         other_narrow = lax.rem(narrow // 2 + 1, 2) * 2 + lax.rem(narrow + core_turn, 2)
         return other_wide, other_narrow, other_narrow * WIDE + other_wide
@@ -402,14 +402,14 @@
 
 
 def gather_parts(real_hbm, imag_hbm, out_hbm, held, load_sem, store_sem):
-    pieces = [(c, row) for row in range(ROWS) for c in range(2)]
+    pieces = [(c, pl.ds(row, 4)) for row in range(0, ROWS, 4) for c in range(2)]
     loads = [
-        pltpu.make_async_copy((real_hbm, imag_hbm)[c].at[row], held.at[c, row], load_sem.at[c, row])
-        for c, row in pieces
+        pltpu.make_async_copy((real_hbm, imag_hbm)[c].at[row], held.at[c, row], load_sem.at[k])
+        for k, (c, row) in enumerate(pieces)
     ]
     stores = [
-        pltpu.make_async_copy(held.at[c, row], out_hbm.at[c, row], store_sem.at[c, row])
-        for c, row in pieces
+        pltpu.make_async_copy(held.at[c, row], out_hbm.at[c, row], store_sem.at[k])
+        for k, (c, row) in enumerate(pieces)
     ]
     for load in loads:
         load.start()
@@ -472,8 +472,8 @@
         out_specs=hbm_spec,
         scratch_shapes=[
             pltpu.VMEM((2, ROWS, COLS, N), BF16),
-            pltpu.SemaphoreType.DMA((2, ROWS)),
-            pltpu.SemaphoreType.DMA((2, ROWS)),
+            pltpu.SemaphoreType.DMA((2 * ROWS,)),
+            pltpu.SemaphoreType.DMA((2 * ROWS,)),
         ],
         compiler_params=pltpu.CompilerParams(vmem_limit_bytes=56 << 20),
     )(real, imag)

time: 117 us -> 115 us (0.983)
  Pallas kernels: 115 us -> 113 us
    pallas_call x1, Pallas kernels: 112 us -> 111 us  [local(): pl.pallas_call(kernel, out_shape=[jax.ShapeDtypeStruct((ROWS, COLS, N), B...]
where the time goes in v3:
time: 115 us; the launch traced here: 113 us
  Pallas kernels  113 us (98%)
    pallas_call x1, Pallas kernels, local(): pl.pallas_call(kernel, out_shape=[jax.ShapeDtypeStruct((ROWS, COLS, N), B...  111 us
    pallas_call x1, Pallas kernels, local(): pl.pallas_call(gather_parts, out_shape=jax.ShapeDtypeStruct((2, ROWS, COL...  2.64 us

profile of v3, /device:TPU:9, one launch (start us, length us, event | category | flops | bytes accessed | tf_op | source)
XLA Modules:
  0.0 113.4 jit_solution(17400923184608550914)
XLA Ops:
  0.0 110.8 %shard_map.55 = (bf16[8,128,512]{2,1,0:T(8,128)(2,1)}, bf16[8,128,512]{2,1,0:T(8,128)(2,1)}) custom-call(bf16[2,8,128,512]{3,2,1,0:T(8,128)(2,1)} %field_hbm.1, f32[8,128]{1,0:T(8,128)} %gain_hbm.1, f32[512]{0:T(512)} %phase_hbm.1, bf16[2,512,512]{2,1,0:T(8,128)(2,1)} %constant.4.clone.table_hbm, f32[512,8,128]{2,1,0:T(8,128)} %constant.5.clone.lines_hbm), custom_call_target="tpu_custom_call" | custom-call | tf_op jit(solution)/shard_map/pallas_call | solution.py:425
  110.8 2.6 %shard_map.56 = bf16[2,8,128,512]{3,2,1,0:T(8,128)(2,1)} custom-call(bf16[8,128,512]{2,1,0:T(8,128)(2,1)} %get-tuple-element.7.real_hbm, bf16[8,128,512]{2,1,0:T(8,128)(2,1)} %get-tuple-element.8.imag_hbm), custom_call_target="tpu_custom_call" | custom-call | tf_op jit(solution)/shard_map/pallas_call | solution.py:468

commit v4 on v3

--- a/solution.py
+++ b/solution.py
@@ -195,7 +195,7 @@
         other_x = lax.rem(wide // 32 + turn, 2)
         other_z = lax.rem(wide // 4 + z_turn, 4) + step // WIDE * 4
         other_wide = other_x * 32 + other_z * 4 + other_y
-        other_narrow = lax.rem(narrow // 2 + 1, 2) * 2 + lax.rem(narrow + core_turn, 2)
+        other_narrow = lax.rem(narrow // 2 + 1, 2) * 2 + 1 - core_turn
         return other_wide, other_narrow, other_narrow * WIDE + other_wide
 
     def send_spectrum(part):

time: 115 us -> 115 us (level)
  no operation moved by 1% of the time
where the time goes in v4:
time: 115 us; the launch traced here: 113 us
  Pallas kernels  113 us (98%)
    pallas_call x1, Pallas kernels, local(): pl.pallas_call(kernel, out_shape=[jax.ShapeDtypeStruct((ROWS, COLS, N), B...  111 us
    pallas_call x1, Pallas kernels, local(): pl.pallas_call(gather_parts, out_shape=jax.ShapeDtypeStruct((2, ROWS, COL...  2.64 us

profile of v4, /device:TPU:9, one launch (start us, length us, event | category | flops | bytes accessed | tf_op | source)
XLA Modules:
  0.0 113.4 jit_solution(6137282587872174221)
XLA Ops:
  0.0 110.7 %shard_map.55 = (bf16[8,128,512]{2,1,0:T(8,128)(2,1)}, bf16[8,128,512]{2,1,0:T(8,128)(2,1)}) custom-call(bf16[2,8,128,512]{3,2,1,0:T(8,128)(2,1)} %field_hbm.1, f32[8,128]{1,0:T(8,128)} %gain_hbm.1, f32[512]{0:T(512)} %phase_hbm.1, bf16[2,512,512]{2,1,0:T(8,128)(2,1)} %constant.4.clone.table_hbm, f32[512,8,128]{2,1,0:T(8,128)} %constant.5.clone.lines_hbm), custom_call_target="tpu_custom_call" | custom-call | tf_op jit(solution)/shard_map/pallas_call | solution.py:425
  110.7 2.6 %shard_map.56 = bf16[2,8,128,512]{3,2,1,0:T(8,128)(2,1)} custom-call(bf16[8,128,512]{2,1,0:T(8,128)(2,1)} %get-tuple-element.7.real_hbm, bf16[8,128,512]{2,1,0:T(8,128)(2,1)} %get-tuple-element.8.imag_hbm), custom_call_target="tpu_custom_call" | custom-call | tf_op jit(solution)/shard_map/pallas_call | solution.py:468
